TPU v7x, 32 devices: a whole 2x2x4 slice. The times are simulated.
32 devices in a mesh: row: 8 (over z, core), col: 4 (over y, x).
Axes of the slice: x: 2, y: 2, z: 4, core: 2. Of those that a mesh axis runs over, the one named last changes fastest.
Arguments:
- inputs: bfloat16 [64, 8192], P('col', 'row'), may hold values from -6 to 6
- w_up: bfloat16 [8192, 26624], P('row', 'col'), may hold values from -0.0625 to 0.0625
- w_down: bfloat16 [26624, 8192], P('col', 'row'), may hold values from -0.0390625 to 0.0390625
- out_grad: bfloat16 [64, 8192], P('col', 'row'), may hold values from -6 to 6
Outputs:
- result: bfloat16 [64, 8192], P('col', 'row')
- in_grad: bfloat16 [64, 8192], P('col', 'row')
- up_grad: bfloat16 [8192, 26624], P('row', 'col')
- down_grad: bfloat16 [26624, 8192], P('col', 'row')
All inputs are finite; a program needn't handle non-finite values.
Results may differ from a plain program's by a relative error of at most 0.005.
Values may be sent and summed in bfloat16 or wider, within the bound.
A program may use at most 128 MiB of HBM per device.

v0:
```python
import jax
import jax.numpy as jnp
from jax import lax
from jax.sharding import PartitionSpec as P


def gelu_value(hidden):
    return 0.5 * hidden * (1.0 + jax.scipy.special.erf(hidden * 0.7071067811865476))


def gelu_slope(hidden):
    return (
        0.5 * (1.0 + jax.scipy.special.erf(hidden * 0.7071067811865476))
        + hidden * jnp.exp(-0.5 * hidden * hidden) * 0.3989422804014327
    )


def contract_first(left, right):
    return lax.dot_general(
        left, right, (((0,), (0,)), ((), ())), preferred_element_type=jnp.float32
    )


def contract_last(left, right):
    return lax.dot_general(
        left, right, (((1,), (1,)), ((), ())), preferred_element_type=jnp.float32
    )


def on_device(inputs, w_up, w_down, out_grad):
    gathered = lax.all_gather(inputs, "col", axis=0, tiled=True)
    cotangent = lax.all_gather(out_grad, "col", axis=0, tiled=True)
    block = gathered
    hidden = lax.psum_scatter(
        jnp.dot(block, w_up, preferred_element_type=jnp.float32),
        "row",
        scatter_dimension=0,
        tiled=True,
    )
    activated_share = gelu_value(hidden).astype(jnp.bfloat16)
    activated = lax.all_gather(activated_share, "row", axis=0, tiled=True)
    block = cotangent
    act_grad = lax.psum_scatter(
        contract_last(block, w_down), "row", scatter_dimension=0, tiled=True
    )
    grad_share = (act_grad * gelu_slope(hidden)).astype(jnp.bfloat16)
    hid_grad = lax.all_gather(grad_share, "row", axis=0, tiled=True)
    block = activated
    result = lax.psum_scatter(
        jnp.dot(block, w_down, preferred_element_type=jnp.float32),
        "col",
        scatter_dimension=0,
        tiled=True,
    ).astype(jnp.bfloat16)
    down_grad = contract_first(activated, cotangent).astype(jnp.bfloat16)
    block = hid_grad
    in_grad = lax.psum_scatter(
        contract_last(block, w_up), "col", scatter_dimension=0, tiled=True
    ).astype(jnp.bfloat16)
    up_grad = contract_first(gathered, hid_grad).astype(jnp.bfloat16)
    return (result, in_grad, up_grad, down_grad)


def solution(mesh):
    return jax.shard_map(
        on_device,
        mesh=mesh,
        in_specs=(P("col", "row"), P("row", "col"), P("col", "row"), P("col", "row")),
        out_specs=(P("col", "row"), P("col", "row"), P("row", "col"), P("col", "row")),
        check_vma=False,
    )
```

profile of v0, /device:TPU:0, one launch (start us, length us, event | category | flops | bytes accessed | tf_op | source)
XLA Modules:
  0.0 190.8 jit_solution(13815074010332645011)
XLA Ops:
  7.2 0.0 copy-start
  7.2 0.0 reduce-scatter.9.cloned.1.call-start
  7.2 10.1 %all_gather.14 = bf16[64,1024]{1,0:T(8,128)(2,1)S(1)} all-gather(bf16[16,1024]{1,0:T(8,128)(2,1)} %param.7), channel_id=1, replica_groups=mesh['row'=8,'col'=4] {'col'}, dimensions={0}, use_global_device_ids=true | all-gather | bytes 163840 | tf_op jit(solution)/shard_map/all_gather | solution.py:32
  17.3 10.3 %fusion.8 = f32[64,6656]{1,0:T(8,128)} fusion(bf16[64,1024]{1,0:T(8,128)(2,1)S(1)} %all_gather.14, bf16[6656,1024]{1,0:T(8,128)(2,1)} %param.6), kind=kOutput, calls=%fused_computation.13 | convolution fusion | flops 872415232 | bytes 15466496 | tf_op jit(solution)/shard_map/dot_general | solution.py:25
  27.6 0.0 reduce-scatter.9.cloned.1.call-update
  27.7 0.0 reduce-scatter.5.cloned.1.call-start
  27.7 0.0 copy-done
  27.7 8.3 %all_gather.12 = bf16[64,1024]{1,0:T(8,128)(2,1)S(1)} all-gather(bf16[16,1024]{1,0:T(8,128)(2,1)S(1)} %copy-done), channel_id=1, replica_groups=mesh['row'=8,'col'=4] {'col'}, dimensions={0}, use_global_device_ids=true | all-gather | bytes 163840 | tf_op jit(solution)/shard_map/all_gather | solution.py:31
  36.0 8.6 %fusion.6 = f32[64,6656]{1,0:T(8,128)} fusion(bf16[64,1024]{1,0:T(8,128)(2,1)S(1)} %all_gather.12, bf16[1024,6656]{1,0:T(8,128)(2,1)} %param.5), kind=kOutput, calls=%fused_computation.11 | convolution fusion | flops 872415232 | bytes 15466496 | tf_op jit(solution)/shard_map/dot_general | solution.py:35
  44.6 0.0 reduce-scatter.5.cloned.1.call-update
  44.6 0.0 reduce-scatter.7.cloned.1.call-start
  44.6 18.2 %reduce-scatter.9.cloned.1.call-done = f32[8,6656]{1,0:T(8,128)} async-done(((f32[64,6656]{1,0:T(8,128)}), f32[8,6656]{1,0:T(8,128)}) %reduce-scatter.9.cloned.1.call-update) | async-done | bytes 213008 | tf_op jit(solution)/shard_map/reduce_scatter | solution.py:43
  62.8 35.7 %reduce-scatter.5.cloned.1.call-done = f32[8,6656]{1,0:T(8,128)} async-done(((f32[64,6656]{1,0:T(8,128)}), f32[8,6656]{1,0:T(8,128)}) %reduce-scatter.5.cloned.1.call-update) | async-done | bytes 213008 | tf_op jit(solution)/shard_map/reduce_scatter | solution.py:34
  98.5 1.1 fusion.5
  99.6 15.8 %all_gather.13 = bf16[64,6656]{1,0:T(8,128)(2,1)S(1)} all-gather(bf16[8,6656]{1,0:T(8,128)(2,1)S(1)} %get-tuple-element.9), channel_id=1, replica_groups=mesh['row'=8,'col'=4] {'row'}, dimensions={0}, use_global_device_ids=true | all-gather | bytes 958464 | tf_op jit(solution)/shard_map/all_gather | solution.py:41
  115.4 8.1 %fusion.7 = f32[64,1024]{1,0:T(8,128)} fusion(bf16[64,6656]{1,0:T(8,128)(2,1)S(1)} %all_gather.13, bf16[6656,1024]{1,0:T(8,128)(2,1)} %param.6), kind=kOutput, calls=%fused_computation.12 | convolution fusion | flops 872415232 | bytes 14745600 | tf_op jit(solution)/shard_map/dot_general | solution.py:50
  123.5 0.0 reduce-scatter.7.cloned.1.call-update
  123.5 0.0 reduce-scatter.11.cloned.1.call-start
  123.6 16.5 %all_gather.15 = bf16[64,6656]{1,0:T(8,128)(2,1)S(1)} all-gather(bf16[8,6656]{1,0:T(8,128)(2,1)S(1)} %get-tuple-element.8), channel_id=1, replica_groups=mesh['row'=8,'col'=4] {'row'}, dimensions={0}, use_global_device_ids=true | all-gather | bytes 958464 | tf_op jit(solution)/shard_map/all_gather | solution.py:47
  140.0 6.9 %convert_bitcast_fusion = bf16[1024,6656]{0,1:T(8,128)(2,1)} fusion(bf16[64,6656]{1,0:T(8,128)(2,1)S(1)} %all_gather.15, bf16[64,1024]{1,0:T(8,128)(2,1)S(1)} %all_gather.12), kind=kOutput, calls=%fused_computation | convolution fusion | flops 879230976 | bytes 14614528 | tf_op jit(solution)/shard_map/dot_general | solution.py:19
  146.9 9.8 %fusion.9 = f32[64,1024]{1,0:T(8,128)} fusion(bf16[64,6656]{1,0:T(8,128)(2,1)S(1)} %all_gather.15, bf16[1024,6656]{1,0:T(8,128)(2,1)} %param.5), kind=kOutput, calls=%fused_computation.14 | convolution fusion | flops 872415232 | bytes 14745600 | tf_op jit(solution)/shard_map/dot_general | solution.py:25
  156.7 0.0 reduce-scatter.11.cloned.1.call-update
  156.7 7.1 %convolution_convert_fusion = bf16[6656,1024]{1,0:T(8,128)(2,1)} fusion(bf16[64,6656]{1,0:T(8,128)(2,1)S(1)} %all_gather.13, bf16[64,1024]{1,0:T(8,128)(2,1)S(1)} %all_gather.14), kind=kOutput, calls=%fused_computation.1 | convolution fusion | flops 879230976 | bytes 14614528 | tf_op jit(solution)/shard_map/dot_general | solution.py:19
  163.8 17.5 %copy.8 = bf16[1024,6656]{1,0:T(8,128)(2,1)} copy(bf16[1024,6656]{0,1:T(8,128)(2,1)} %convert_bitcast_fusion) | data formatting | bytes 27262976
  181.3 0.0 reduce-scatter.7.cloned.1.call-done
  181.3 1.5 convert_element_type.22
  182.8 0.0 reduce-scatter.11.cloned.1.call-done
  182.8 1.5 convert_element_type.24
Async XLA Ops:
  7.2 20.6 %copy-start = (bf16[16,1024]{1,0:T(8,128)(2,1)S(1)}, bf16[16,1024]{1,0:T(8,128)(2,1)}, u32[]{:S(2)}) copy-start(bf16[16,1024]{1,0:T(8,128)(2,1)} %param.4) | copy-start | bytes 98308
  7.2 55.6 %reduce-scatter.9.cloned.1.call-start = ((), (), s32[]{:S(2)}) async-start(), calls=%async_computation.6 | async-start | bytes 1916928 | tf_op jit(solution)/shard_map/reduce_scatter | solution.py:43
  27.7 70.8 %reduce-scatter.5.cloned.1.call-start = ((), (), s32[]{:S(2)}) async-start(), calls=%async_computation.4 | async-start | bytes 1916928 | tf_op jit(solution)/shard_map/reduce_scatter | solution.py:34
  44.6 136.7 %reduce-scatter.7.cloned.1.call-start = ((), (), s32[]{:S(2)}) async-start(), calls=%async_computation.5 | async-start | bytes 327680 | tf_op jit(solution)/shard_map/reduce_scatter | solution.py:49
  123.5 59.2 %reduce-scatter.11.cloned.1.call-start = ((), (), s32[]{:S(2)}) async-start(), calls=%async_computation.7 | async-start | bytes 327680 | tf_op jit(solution)/shard_map/reduce_scatter | solution.py:57
Sparse Core Ops, SparseCore 0:
  27.8 34.9 reduce-scatter.8
  65.8 32.6 reduce-scatter.4
  123.6 22.4 reduce-scatter.6
  156.8 22.2 reduce-scatter.10
where the time goes:
time: 192 us; the launch traced here: 191 us
  waiting for transfers between devices  53.9 us (28%)
  blocking collectives  50.7 us (26%)
  matrix products  50.7 us (26%)
  local copies, waits for them, and re-layouts  17.5 us (9%)
  between operations  13.8 us (7%)
  other arithmetic  4.06 us (2%)
    reduce_scatter x1, waiting for transfers between devices, on_device(): lax.psum_scatter(jnp.dot(block, w_up, preferred_element_type=jnp.float32)...  35.7 us
    dot_general x2, matrix products, contract_last(): lax.dot_general(left, right, (((1,), (1,)), ((), ())), preferred_element_...  20.1 us
    reduce_scatter x1, waiting for transfers between devices, on_device(): lax.psum_scatter(contract_last(block, w_down), 'row', scatter_dimension=0...  18.2 us
    unnamed x3, local copies, waits for them, and re-layouts  17.5 us
    all_gather x1, blocking collectives, on_device(): hid_grad = lax.all_gather(grad_share, 'row', axis=0, tiled=True)  16.5 us
    all_gather x1, blocking collectives, on_device(): activated = lax.all_gather(activated_share, 'row', axis=0, tiled=True)  15.8 us
    dot_general x2, matrix products, contract_first(): lax.dot_general(left, right, (((0,), (0,)), ((), ())), preferred_element_...  14 us
    all_gather x1, blocking collectives, on_device(): cotangent = lax.all_gather(out_grad, 'col', axis=0, tiled=True)  10.1 us
  transfers between devices with their start and end apart: 4, of which 2 were waited for; matrix products, arithmetic and copies ran while one was open for 27% of the time, Pallas kernels for 0%

commit v1 on v0

v1 whole, which is shorter than its diff:
```python
import functools

import jax
import jax.numpy as jnp
from jax import lax
from jax.experimental import pallas as pl
from jax.experimental.pallas import tpu as pltpu
from jax.sharding import PartitionSpec as P

MESH = pl.DeviceIdType.MESH
F32 = jnp.float32
BF16 = jnp.bfloat16


def gelu_value(hidden):
    return 0.5 * hidden * (1.0 + lax.erf(hidden * 0.7071067811865476))


def gelu_slope(hidden):
    return (
        0.5 * (1.0 + lax.erf(hidden * 0.7071067811865476))
        + hidden * jnp.exp(-0.5 * hidden * hidden) * 0.3989422804014327
    )


def contract_first(left, right):
    return lax.dot_general(
        left, right, (((0,), (0,)), ((), ())), preferred_element_type=F32
    )


def contract_last(left, right):
    return lax.dot_general(
        left, right, (((1,), (1,)), ((), ())), preferred_element_type=F32
    )


def tile_of(size):
    return 256 if size % 256 == 0 else 128


def tiles(size, body):
    tile = tile_of(size)

    @pl.loop(0, size // tile)
    def _(step):
        body(pl.ds(pl.multiple_of(step * tile, tile), tile))


def exchange_kernel(
    R, C,
    x_ref, wup_ref, wdn_ref, g_ref,
    res_ref, ing_ref, act_ref, hg_ref, xo_ref, go_ref,
    wup, wdn, xg, pair_send, pair_recv, own, zsend, zrecv, hid, half, part, csend, crecv,
    w_sem, ag_s, ag_r, pr_s, pr_r, zs_s, zs_r, za_s, za_r, sb_s, sb_r, co_s, co_r,
):
    Z = R // 2
    r, c = lax.axis_index("row"), lax.axis_index("col")
    z, core = lax.div(r, 2), lax.rem(r, 2)
    other = 1 - core
    TC, K = x_ref.shape
    T = TC * C
    TG = T // Z
    F = wup_ref.shape[1]
    W = wup.shape[2]
    skip = 2 * W - F

    def zpeer(k):
        return {"row": lax.rem(z + k, Z) * 2 + core}

    def cpeer(k):
        return {"col": lax.rem(c + k, C)}

    sibling = {"row": z * 2 + other}

    def zrows(k):
        return pl.ds(pl.multiple_of(lax.rem(z + k, Z) * TG, TG), TG)

    def crows(k):
        return pl.ds(pl.multiple_of(lax.rem(c + k, C) * TC, TC), TC)

    def remote(src, dst, ssem, rsem, peer):
        return pltpu.make_async_remote_copy(
            src_ref=src, dst_ref=dst, send_sem=ssem, recv_sem=rsem,
            device_id=peer, device_id_type=MESH,
        )

    def load(op, which):
        start = pl.multiple_of(which * (F - W), 128)
        if op == 0:
            src, dst = wup_ref.at[:, pl.ds(start, W)], wup.at[which]
        else:
            src, dst = wdn_ref.at[pl.ds(start, W), :], wdn.at[which]
        return pltpu.make_async_copy(src, dst, w_sem.at[op, which])

    loads = {}
    for op in range(2):
        for name, which in (("other", other), ("own", core)):
            loads[op, name] = load(op, which)
            loads[op, name].start()

    barrier = pltpu.get_barrier_semaphore()
    peers = [sibling] + [zpeer(k) for k in range(1, Z)] + [cpeer(k) for k in range(1, C)]
    for peer in peers:
        pl.semaphore_signal(barrier, inc=1, device_id=peer, device_id_type=MESH)
    pl.semaphore_wait(barrier, len(peers))

    sends = []

    gathers = []
    for op, ref in enumerate((x_ref, g_ref)):
        for k in range(1, C):
            copy = remote(ref, xg.at[op, crows(0)], ag_s.at[op, k], ag_r.at[op, k], cpeer(k))
            copy.start()
            gathers.append((op, copy))
            sends.append(copy)
        xg[op, crows(0), :] = ref[...]

    def partial(op, which, cols):
        if op == 0:
            return jnp.dot(xg[0], wup[which, :, cols], preferred_element_type=F32)
        return contract_last(xg[1], wdn[which, cols, :])

    zsums = {}
    for op in range(2):
        for o, copy in gathers:
            if o == op:
                copy.wait_recv()
        loads[op, "other"].wait()

        def to_send(cols, op=op):
            pair_send[op, :, cols] = partial(op, other, cols).astype(BF16)

        tiles(W, to_send)
        pair = remote(pair_send.at[op], pair_recv.at[op], pr_s.at[op], pr_r.at[op], sibling)
        pair.start()
        sends.append(pair)
        loads[op, "own"].wait()

        def to_keep(cols, op=op):
            own[op, :, cols] = partial(op, core, cols)

        tiles(W, to_keep)
        pair.wait_recv()

        def add_pair(cols, op=op):
            total = own[op, :, cols] + pair_recv[op, :, cols].astype(F32)
            own[op, :, cols] = total
            zsend[op, :, cols] = total.astype(BF16)

        tiles(W, add_pair)
        for k in range(1, Z):
            copy = remote(
                zsend.at[op, zrows(k)], zrecv.at[op, k - 1],
                zs_s.at[op, k], zs_r.at[op, k], zpeer(k),
            )
            copy.start()
            zsums[op, k] = copy
            sends.append(copy)

    spread, shared = {}, {}
    for op in range(2):
        for k in range(1, Z):
            zsums[op, k].wait_recv()

        def share(cols, op=op):
            total = own[op, zrows(0), cols]
            for k in range(1, Z):
                total = total + zrecv[op, k - 1, :, cols].astype(F32)
            if op == 0:
                hid[:, cols] = total
                total = gelu_value(total)
            else:
                total = total * gelu_slope(hid[:, cols])
            half[op, core, zrows(0), cols] = total.astype(BF16)

        tiles(W, share)
        for k in range(1, Z):
            block = half.at[op, core, zrows(0)]
            copy = remote(block, block, za_s.at[op, k], za_r.at[op, k], zpeer(k))
            copy.start()
            spread[op, k] = copy
            sends.append(copy)
        block = half.at[op, core, zrows(0)]
        copy = remote(block, block, sb_s.at[op, 0], sb_r.at[op, 0], sibling)
        copy.start()
        shared[op, 0] = copy
        sends.append(copy)

    outs = {}
    for op in range(2):
        for k in range(1, Z):
            spread[op, k].wait_recv()
            block = half.at[op, core, zrows(Z - k)]
            copy = remote(block, block, sb_s.at[op, k], sb_r.at[op, k], sibling)
            copy.start()
            shared[op, k] = copy
            sends.append(copy)
        for k in range(Z):
            shared[op, k].wait_recv()

        def project(cols, op=op):
            if op == 0:
                total = jnp.dot(half[0, 0], wdn[0, :, cols], preferred_element_type=F32)
                total += jnp.dot(
                    half[0, 1, :, skip:], wdn[1, skip:, cols], preferred_element_type=F32
                )
            else:
                total = contract_last(half[1, 0], wup[0, cols, :])
                total += contract_last(half[1, 1, :, skip:], wup[1, cols, skip:])
            part[op, :, cols] = total
            csend[op, :, cols] = total.astype(BF16)

        tiles(K, project)
        for k in range(1, C):
            copy = remote(
                csend.at[op, crows(k)], crecv.at[op, k - 1],
                co_s.at[op, k], co_r.at[op, k], cpeer(k),
            )
            copy.start()
            outs[op, k] = copy
            sends.append(copy)

    for op, ref in enumerate((act_ref, hg_ref)):
        ref[:, :W] = half[op, 0]
        ref[:, W:] = half[op, 1, :, skip:]
    xo_ref[...] = xg[0]
    go_ref[...] = xg[1]

    for op, ref in enumerate((res_ref, ing_ref)):
        total = part[op, crows(0), :]
        for k in range(1, C):
            outs[op, k].wait_recv()
            total = total + crecv[op, k - 1].astype(F32)
        ref[...] = total.astype(ref.dtype)

    for copy in sends:
        copy.wait_send()


def on_device(R, C, inputs, w_up, w_down, out_grad):
    TC, K = inputs.shape
    F = w_up.shape[1]
    T, Z = TC * C, R // 2
    TG = T // Z
    W = -(-F // 256) * 128
    vmem = pl.BlockSpec(memory_space=pltpu.VMEM)
    hbm = pl.BlockSpec(memory_space=pl.ANY)
    dma = pltpu.SemaphoreType.DMA
    shape = jax.ShapeDtypeStruct
    result, in_grad, activated, hid_grad, gathered, cotangent = pl.pallas_call(
        functools.partial(exchange_kernel, R, C),
        out_shape=[
            shape((TC, K), BF16), shape((TC, K), BF16),
            shape((T, F), BF16), shape((T, F), BF16),
            shape((T, K), BF16), shape((T, K), BF16),
        ],
        in_specs=[vmem, hbm, hbm, vmem],
        out_specs=[vmem] * 6,
        scratch_shapes=[
            pltpu.VMEM((2, K, W), BF16),
            pltpu.VMEM((2, W, K), BF16),
            pltpu.VMEM((2, T, K), BF16),
            pltpu.VMEM((2, T, W), BF16),
            pltpu.VMEM((2, T, W), BF16),
            pltpu.VMEM((2, T, W), F32),
            pltpu.VMEM((2, T, W), BF16),
            pltpu.VMEM((2, Z - 1, TG, W), BF16),
            pltpu.VMEM((TG, W), F32),
            pltpu.VMEM((2, 2, T, W), BF16),
            pltpu.VMEM((2, T, K), F32),
            pltpu.VMEM((2, T, K), BF16),
            pltpu.VMEM((2, C - 1, TC, K), BF16),
            dma((2, 2)),
            dma((2, C)), dma((2, C)),
            dma((2,)), dma((2,)),
            dma((2, Z)), dma((2, Z)),
            dma((2, Z)), dma((2, Z)),
            dma((2, Z)), dma((2, Z)),
            dma((2, C)), dma((2, C)),
        ],
        compiler_params=pltpu.CompilerParams(
            collective_id=0, has_side_effects=True, vmem_limit_bytes=56 * 2**20
        ),
        cost_estimate=pl.CostEstimate(
            flops=8 * T * K * F, bytes_accessed=4 * K * F, transcendentals=0
        ),
    )(inputs, w_up, w_down, out_grad)
    down_grad = contract_first(activated, cotangent).astype(BF16)
    up_grad = contract_first(gathered, hid_grad).astype(BF16)
    return (result, in_grad, up_grad, down_grad)


def solution(mesh):
    R, C = mesh.shape["row"], mesh.shape["col"]
    return jax.shard_map(
        functools.partial(on_device, R, C),
        mesh=mesh,
        in_specs=(P("col", "row"), P("row", "col"), P("col", "row"), P("col", "row")),
        out_specs=(P("col", "row"), P("col", "row"), P("row", "col"), P("col", "row")),
        check_vma=False,
    )
```

time: 192 us -> 82.5 us (0.43)
  Pallas kernels: 0 us -> 62.4 us
  waiting for transfers between devices: 53.9 us -> 0 us
  blocking collectives: 50.7 us -> 0 us
  matrix products: 50.7 us -> 17.3 us
  local copies, waits for them, and re-layouts: 17.5 us -> 1.25 us
  between operations: 13.8 us -> 0.67 us
  other arithmetic: 4.06 us -> 0 us
    pallas_call x0 -> x1, Pallas kernels: none -> 62.4 us  [on_device(): pl.pallas_call(functools.partial(exchange_kernel, R, C), out_shape=[shape...]
    reduce_scatter x4 -> x0, waiting for transfers between devices: 53.9 us -> none  [the longest x1 35.7 us: on_device(): lax.psum_scatter(jnp.dot(block, w_up, preferred_element_type=jnp.float32)...]
    all_gather x4 -> x0, blocking collectives: 50.7 us -> none  [the longest x1 16.5 us: on_device(): hid_grad = lax.all_gather(grad_share, 'row', axis=0, tiled=True)]
    dot_general x4 -> x0, matrix products: 36.7 us -> none  [the longest x2 20.1 us: contract_last(): lax.dot_general(left, right, (((1,), (1,)), ((), ())), preferred_element_...]
    unnamed x3 -> x10, local copies, waits for them, and re-layouts: 17.5 us -> 1.25 us
    convert_element_type x3 -> x0, other arithmetic: 4.06 us -> none  [the longest x1 1.46 us: on_device(): result = lax.psum_scatter(jnp.dot(block, w_down, preferred_element_type=j...]
    dot_general x2, matrix products: 14 us -> 17.3 us  [contract_first(): lax.dot_general(left, right, (((0,), (0,)), ((), ())), preferred_element_...]
  transfers between devices with their start and end apart: 4 -> 0, of which waited for: 2 -> 0; matrix products, arithmetic and copies ran while one was open for 27% -> 0% of each run, Pallas kernels for 0% -> 0%
where the time goes in v1:
time: 82.5 us; the launch traced here: 81.6 us
  Pallas kernels  62.4 us (76%)
  matrix products  17.3 us (21%)
  local copies, waits for them, and re-layouts  1.25 us (2%)
    pallas_call x1, Pallas kernels, on_device(): pl.pallas_call(functools.partial(exchange_kernel, R, C), out_shape=[shape...  62.4 us
    dot_general x2, matrix products, contract_first(): lax.dot_general(left, right, (((0,), (0,)), ((), ())), preferred_element_...  17.3 us

profile of v1, /device:TPU:0, one launch (start us, length us, event | category | flops | bytes accessed | tf_op | source)
XLA Modules:
  0.0 81.6 jit_solution(6154478170038892069)
XLA Ops:
  0.6 62.4 %shard_map.75 = (bf16[16,1024]{1,0:T(8,128)(2,1)}, bf16[16,1024]{1,0:T(8,128)(2,1)}, bf16[64,6656]{1,0:T(8,128)(2,1)}, bf16[64,6656]{1,0:T(8,128)(2,1)}, bf16[64...) custom-call(bf16[16,1024]{1,0:T(8,128)(2,1)} %x_ref.1, bf16[1024,6656]{1,0:T(8,128)(2,1)} %wup_ref.1, ...), custom_call_target="tpu_custom_call" | custom-call | flops 3489660928 | bytes 27262976 | tf_op jit(solution)/shard_map/pallas_call | solution.py:251
  63.1 0.0 copy-start
  63.1 0.0 copy-start.1
  63.1 10.2 %convolution_convert_fusion.1 = bf16[1024,6656]{1,0:T(8,128)(2,1)} fusion(bf16[64,1024]{1,0:T(8,128)(2,1)} %get-tuple-element.12, bf16[64,6656]{1,0:T(8,128)(2,1)} %get-tuple-element.13), kind=kOutput, calls=%fused_computation.1 | convolution fusion | flops 879230976 | bytes 14614528 | tf_op jit(solution)/shard_map/dot_general | solution.py:27
  73.2 0.0 copy-done
  73.2 0.0 copy-done.1
  73.2 0.0 copy-start.3
  73.2 0.0 copy-start.2
  73.3 7.1 %convolution_convert_fusion = bf16[6656,1024]{1,0:T(8,128)(2,1)} fusion(bf16[64,6656]{1,0:T(8,128)(2,1)S(1)} %copy-done, bf16[64,1024]{1,0:T(8,128)(2,1)S(1)} %copy-done.1), kind=kOutput, calls=%fused_computation | convolution fusion | flops 879230976 | bytes 14614528 | tf_op jit(solution)/shard_map/dot_general | solution.py:27
  80.4 0.0 copy-done.3
  80.4 0.6 copy.10
  81.0 0.0 copy-done.2
  81.0 0.6 copy.11
Async XLA Ops:
  63.1 10.2 %copy-start = (bf16[64,6656]{1,0:T(8,128)(2,1)S(1)}, bf16[64,6656]{1,0:T(8,128)(2,1)}, u32[]{:S(2)}) copy-start(bf16[64,6656]{1,0:T(8,128)(2,1)} %get-tuple-element.14) | copy-start | bytes 2555908
  63.1 10.2 %copy-start.1 = (bf16[64,1024]{1,0:T(8,128)(2,1)S(1)}, bf16[64,1024]{1,0:T(8,128)(2,1)}, u32[]{:S(2)}) copy-start(bf16[64,1024]{1,0:T(8,128)(2,1)} %get-tuple-element.15) | copy-start | bytes 393220
  73.2 7.1 %copy-start.3 = (bf16[16,1024]{1,0:T(8,128)(2,1)S(1)}, bf16[16,1024]{1,0:T(8,128)(2,1)}, u32[]{:S(2)}) copy-start(bf16[16,1024]{1,0:T(8,128)(2,1)} %get-tuple-element.20) | copy-start | bytes 98308
  73.2 7.7 %copy-start.2 = (bf16[16,1024]{1,0:T(8,128)(2,1)S(1)}, bf16[16,1024]{1,0:T(8,128)(2,1)}, u32[]{:S(2)}) copy-start(bf16[16,1024]{1,0:T(8,128)(2,1)} %get-tuple-element.21) | copy-start | bytes 98308

commit v2 on v1

--- a/solution.py
+++ b/solution.py
@@ -236,6 +236,35 @@
 
     for copy in sends:
         copy.wait_send()
+
+
+def grads_kernel(x_ref, h_ref, a_ref, g_ref, up_ref, down_ref):
+    up_ref[...] = contract_first(x_ref[...], h_ref[...]).astype(BF16)
+    down_ref[...] = contract_first(a_ref[...], g_ref[...]).astype(BF16)
+
+
+def weight_grads(gathered, hid_grad, activated, cotangent):
+    T, K = gathered.shape
+    F = hid_grad.shape[1]
+    tile = 512 if F % 512 == 0 else 128
+    whole = pl.BlockSpec((T, K), lambda i: (0, 0))
+    piece = pl.BlockSpec((T, tile), lambda i: (0, i))
+    return pl.pallas_call(
+        grads_kernel,
+        grid=(F // tile,),
+        out_shape=[
+            jax.ShapeDtypeStruct((K, F), BF16), jax.ShapeDtypeStruct((F, K), BF16),
+        ],
+        in_specs=[whole, piece, piece, whole],
+        out_specs=[
+            pl.BlockSpec((K, tile), lambda i: (0, i)),
+            pl.BlockSpec((tile, K), lambda i: (i, 0)),
+        ],
+        compiler_params=pltpu.CompilerParams(vmem_limit_bytes=40 * 2**20),
+        cost_estimate=pl.CostEstimate(
+            flops=4 * T * K * F, bytes_accessed=4 * K * F, transcendentals=0
+        ),
+    )(gathered, hid_grad, activated, cotangent)
 
 
 def on_device(R, C, inputs, w_up, w_down, out_grad):
@@ -286,8 +315,7 @@
             flops=8 * T * K * F, bytes_accessed=4 * K * F, transcendentals=0
         ),
     )(inputs, w_up, w_down, out_grad)
-    down_grad = contract_first(activated, cotangent).astype(BF16)
-    up_grad = contract_first(gathered, hid_grad).astype(BF16)
+    up_grad, down_grad = weight_grads(gathered, hid_grad, activated, cotangent)
     return (result, in_grad, up_grad, down_grad)
 
 

time: 82.5 us -> 83.4 us (1.011)
  matrix products: 17.3 us -> 0 us
  Pallas kernels: 62.4 us -> 74.8 us
  local copies, waits for them, and re-layouts: 1.25 us -> 6.86 us
    dot_general x2 -> x0, matrix products: 17.3 us -> none  [contract_first(): lax.dot_general(left, right, (((0,), (0,)), ((), ())), preferred_element_...]
    pallas_call x0 -> x1, Pallas kernels: none -> 12.3 us  [weight_grads(): pl.pallas_call(grads_kernel, grid=(F // tile,), out_shape=[jax.ShapeDtype...]
    unnamed x10, local copies, waits for them, and re-layouts: 1.25 us -> 6.86 us
where the time goes in v2:
time: 83.4 us; the launch traced here: 82.3 us
  Pallas kernels  74.8 us (90%)
  local copies, waits for them, and re-layouts  6.86 us (8%)
    pallas_call x1, Pallas kernels, on_device(): pl.pallas_call(functools.partial(exchange_kernel, R, C), out_shape=[shape...  62.4 us
    pallas_call x1, Pallas kernels, weight_grads(): pl.pallas_call(grads_kernel, grid=(F // tile,), out_shape=[jax.ShapeDtype...  12.3 us
    unnamed x10, local copies, waits for them, and re-layouts  6.86 us

profile of v2, /device:TPU:0, one launch (start us, length us, event | category | flops | bytes accessed | tf_op | source)
XLA Modules:
  0.0 82.3 jit_solution(11041426832484978896)
XLA Ops:
  0.6 62.4 %shard_map.75 = (bf16[16,1024]{1,0:T(8,128)(2,1)}, bf16[16,1024]{1,0:T(8,128)(2,1)}, bf16[64,6656]{1,0:T(8,128)(2,1)}, bf16[64,6656]{1,0:T(8,128)(2,1)}, bf16[64...) custom-call(bf16[16,1024]{1,0:T(8,128)(2,1)} %x_ref.1, bf16[1024,6656]{1,0:T(8,128)(2,1)} %wup_ref.1, ...), custom_call_target="tpu_custom_call" | custom-call | flops 3489660928 | bytes 27262976 | tf_op jit(solution)/shard_map/pallas_call | solution.py:280
  63.1 0.0 copy-start
  63.1 1.1 %copy-done = bf16[64,6656]{1,0:T(8,128)(2,1)S(1)} copy-done((bf16[64,6656]{1,0:T(8,128)(2,1)S(1)}, bf16[64,6656]{1,0:T(8,128)(2,1)}, u32[]{:S(2)}) %copy-start) | copy-done | bytes 851992
  64.2 0.0 copy-start.1
  64.2 1.2 %copy-done.1 = bf16[64,6656]{1,0:T(8,128)(2,1)S(1)} copy-done((bf16[64,6656]{1,0:T(8,128)(2,1)S(1)}, bf16[64,6656]{1,0:T(8,128)(2,1)}, u32[]{:S(2)}) %copy-start.1) | copy-done | bytes 851992
  65.4 0.0 copy-start.2
  65.4 0.9 %copy-done.2 = bf16[64,1024]{1,0:T(8,128)(2,1)S(1)} copy-done((bf16[64,1024]{1,0:T(8,128)(2,1)S(1)}, bf16[64,1024]{1,0:T(8,128)(2,1)}, u32[]{:S(2)}) %copy-start.2) | copy-done | bytes 131096
  66.3 0.0 copy-start.3
  66.3 0.9 %copy-done.3 = bf16[64,1024]{1,0:T(8,128)(2,1)S(1)} copy-done((bf16[64,1024]{1,0:T(8,128)(2,1)S(1)}, bf16[64,1024]{1,0:T(8,128)(2,1)}, u32[]{:S(2)}) %copy-start.3) | copy-done | bytes 131096
  67.2 12.3 %shard_map.76 = (bf16[1024,6656]{1,0:T(8,128)(2,1)}, bf16[6656,1024]{1,0:T(8,128)(2,1)}) custom-call(bf16[64,1024]{1,0:T(8,128)(2,1)S(1)} %copy-done.2, bf16[64,6656]{1,0:T(8,128)(2,1)S(1)} %copy-done.1, bf16[64,6656]{1,0:T(8,128)(2,1)S(1)} %copy-done, bf16[64,1024]{1,0:T(8,128)(2,1)S(1)} %copy-done.3), custom_call_target="tpu_custom_call" | custom-call | flops 1744830464 | bytes 27262976 | tf_op jit(solution)/shard_map/pallas_call | solution.py:252
  79.5 1.4 %copy.10 = bf16[16,1024]{1,0:T(8,128)(2,1)} copy(bf16[16,1024]{1,0:T(8,128)(2,1)} %get-tuple-element.24) | data formatting | bytes 65536
  80.9 1.4 %copy.11 = bf16[16,1024]{1,0:T(8,128)(2,1)} copy(bf16[16,1024]{1,0:T(8,128)(2,1)} %get-tuple-element.25) | data formatting | bytes 65536
Async XLA Ops:
  63.1 1.2 %copy-start = (bf16[64,6656]{1,0:T(8,128)(2,1)S(1)}, bf16[64,6656]{1,0:T(8,128)(2,1)}, u32[]{:S(2)}) copy-start(bf16[64,6656]{1,0:T(8,128)(2,1)} %get-tuple-element.16.a_ref) | copy-start | bytes 2555908
  64.2 1.2 %copy-start.1 = (bf16[64,6656]{1,0:T(8,128)(2,1)S(1)}, bf16[64,6656]{1,0:T(8,128)(2,1)}, u32[]{:S(2)}) copy-start(bf16[64,6656]{1,0:T(8,128)(2,1)} %get-tuple-element.15.h_ref) | copy-start | bytes 2555908
  65.4 0.9 %copy-start.2 = (bf16[64,1024]{1,0:T(8,128)(2,1)S(1)}, bf16[64,1024]{1,0:T(8,128)(2,1)}, u32[]{:S(2)}) copy-start(bf16[64,1024]{1,0:T(8,128)(2,1)} %get-tuple-element.14.x_ref) | copy-start | bytes 393220
  66.3 0.9 %copy-start.3 = (bf16[64,1024]{1,0:T(8,128)(2,1)S(1)}, bf16[64,1024]{1,0:T(8,128)(2,1)}, u32[]{:S(2)}) copy-start(bf16[64,1024]{1,0:T(8,128)(2,1)} %get-tuple-element.17.g_ref) | copy-start | bytes 393220
